TPU v7x, 32 devices: a whole 2x2x4 slice. The times are simulated.
32 devices in a mesh: seq: 8 (over z, y), tp: 4 (over x, core).
Axes of the slice: x: 2, y: 2, z: 4, core: 2. Of those that a mesh axis runs over, the one named last changes fastest.
Arguments:
- patches: bfloat16 [32, 196, 768], P('seq', 'tp'), may hold values from -6 to 6
- cls_tokens: bfloat16 [32, 768], P(('seq', 'tp')), may hold values from -6 to 6
- frame_clip: int32 [32], P('seq'), may hold values from 0 to 2, as said below
- norm_gain: float32 [2, 3, 768], replicated, may hold values from 0.5 to 1.5
- norm_bias: float32 [2, 3, 768], replicated, may hold values from -2 to 2
- w_tqkv: bfloat16 [2, 768, 2304], replicated, may hold values from -0.21875 to 0.21875
- w_tproj: bfloat16 [2, 768, 768], replicated, may hold values from -0.4375 to 0.4375
- w_tfc: bfloat16 [2, 768, 768], replicated, may hold values from -0.21875 to 0.21875
- w_sqkv: bfloat16 [2, 768, 2304], replicated, may hold values from -0.21875 to 0.21875
- w_sproj: bfloat16 [2, 768, 768], replicated, may hold values from -0.875 to 0.875
- w_fc1: bfloat16 [2, 768, 3072], P(None, None, 'tp'), may hold values from -0.21875 to 0.21875
- w_fc2: bfloat16 [2, 3072, 768], P(None, 'tp'), may hold values from -0.109375 to 0.109375
- cot_patches: bfloat16 [32, 196, 768], P('seq', 'tp'), may hold values from -6 to 6
- cot_cls: bfloat16 [32, 768], P(('seq', 'tp')), may hold values from -6 to 6
Outputs:
- out_patches: bfloat16 [32, 196, 768], P('seq', 'tp')
- out_cls: bfloat16 [32, 768], P(('seq', 'tp'))
- grad_patches: float32 [32, 196, 768], P('seq', 'tp')
- grad_cls: float32 [32, 768], P(('seq', 'tp'))
- grad_attn: float32 [2, 768, 6912], P(None, 'seq')
- grad_norm: float32 [2, 6, 768], P(None, None, 'seq')
- grad_fc1: float32 [2, 768, 3072], P(None, 'seq', 'tp')
- grad_fc2: float32 [2, 3072, 768], P(None, 'tp', 'seq')
Inputs may be any that keep to these rules, and one draw needn't show every extreme that they name: frame_clip[f] is the clip of frame f; every clip has 8 to 16 frames and one has exactly 16.
All inputs are finite; a program needn't handle non-finite values.
Results may differ from a plain program's by a relative error of at most 0.03.
Values may be sent and summed in bfloat16 or wider, within the bound.
A program may use at most 384 MiB of HBM per device.

v0:
```python
import functools
from collections import namedtuple
from types import SimpleNamespace

import jax
import jax.numpy as jnp
from jax import lax
from jax.experimental import pallas as pl
from jax.experimental.pallas import tpu as pltpu
from jax.sharding import PartitionSpec as P

HEAD_DIM = 64
LAYERS = 2
SLOT = 8
EPS = 1e-06
NEG_FILL = -1e30
MESH = pl.DeviceIdType.MESH
BF = jnp.bfloat16
F32 = jnp.float32
NN = (((1,), (0,)), ((), ()))
NT = (((1,), (1,)), ((), ()))
TN = (((0,), (0,)), ((), ()))
VMEM_LIMIT = 62 * 1024 * 1024
BLOCK = 32

Cfg = namedtuple("Cfg", ["S", "T", "N", "D", "G", "R", "PER", "HS", "ND", "HG", "C", "FW"])


def dot(left, right, dims=NN):
    return lax.dot_general(left, right, dims, preferred_element_type=F32)


def params(cid=None):
    return pltpu.CompilerParams(
        collective_id=cid, has_side_effects=cid is not None, vmem_limit_bytes=VMEM_LIMIT
    )


ANY = pl.BlockSpec(memory_space=pl.ANY)
VM = pl.BlockSpec(memory_space=pltpu.VMEM)


def my_index(cfg):
    return lax.axis_index("seq") * cfg.T + lax.axis_index("tp")


def device(cfg, index):
    return (index // cfg.T, lax.rem(index, cfg.T))


def greet_all(cfg, me):
    barrier = pltpu.get_barrier_semaphore()

    def signal(i, carry):
        pl.semaphore_signal(
            barrier, inc=1, device_id=device(cfg, lax.rem(me + i, cfg.N)), device_id_type=MESH
        )
        return carry

    lax.fori_loop(1, cfg.N, signal, 0)
    pl.semaphore_wait(barrier, cfg.N - 1)


def wait_bytes(ref, sem):
    pltpu.make_async_copy(ref, ref, sem).wait()


def head_pair(ref, rows, width, part, pair):
    start = part * width + pair * 128
    return ref[rows, start : start + 128]


def softmax_rows(query, key, mask):
    scores = jnp.where(mask, dot(query, key, NT), NEG_FILL)
    top = jnp.max(scores, -1, keepdims=True)
    weight = jnp.exp(scores - top)
    return weight * (1.0 / jnp.sum(weight, -1, keepdims=True))


def for_row_blocks(total, step, block):
    if total == step:
        block(0)
    else:

        def body(i, carry):
            block(pl.multiple_of(i * step, step))
            return carry

        lax.fori_loop(0, total // step, body, 0)


def attend(qkv, kcol, krow, write):
    total, width = qkv.shape[0], qkv.shape[1] // 3
    step = total if total <= 256 else 64
    every = slice(0, total)
    lane = lax.broadcasted_iota(jnp.int32, (step, 128), 1) < HEAD_DIM
    zero = jnp.zeros((), BF)

    def block(first):
        rows = pl.ds(first, step)
        mask = kcol[rows, :] == krow[...]
        for pair in range(width // 128):
            query = head_pair(qkv, rows, width, 0, pair) * jnp.asarray(HEAD_DIM**-0.5, BF)
            key = head_pair(qkv, every, width, 1, pair)
            value = head_pair(qkv, every, width, 2, pair)
            prob0 = softmax_rows(jnp.where(lane, query, zero), key, mask).astype(BF)
            prob1 = softmax_rows(jnp.where(lane, zero, query), key, mask).astype(BF)
            write(first, step, pair, jnp.where(lane, dot(prob0, value), dot(prob1, value)))

    for_row_blocks(total, step, block)


def attend_back(qkv, grad, kcol, krow, write, acc, pairs):
    total, width = qkv.shape[0], qkv.shape[1] // 3
    step = total if total <= 256 else 64
    every = slice(0, total)
    lane = lax.broadcasted_iota(jnp.int32, (step, 128), 1) < HEAD_DIM
    lane_all = lax.broadcasted_iota(jnp.int32, (total, 128), 1) < HEAD_DIM
    zero = jnp.zeros((), BF)
    scale = HEAD_DIM**-0.5

    for pair in pairs:

        def block(first, pair=pair):
            rows = pl.ds(first, step)
            mask = kcol[rows, :] == krow[...]
            key = head_pair(qkv, every, width, 1, pair)
            value = head_pair(qkv, every, width, 2, pair)
            query = head_pair(qkv, rows, width, 0, pair) * jnp.asarray(scale, BF)
            out = grad[rows, pair * 128 : pair * 128 + 128]
            dq, dk, dv = [], [], []
            for lower in (True, False):
                own = (lambda v: jnp.where(lane, v, zero)) if lower else (lambda v: jnp.where(lane, zero, v))
                prob = softmax_rows(own(query), key, mask)
                back = dot(own(out), value, NT)
                delta = jnp.sum(prob * back, -1, keepdims=True)
                score = (prob * (back - delta)).astype(BF)
                dq.append(dot(score, key))
                dk.append(dot(score, query, TN))
                dv.append(dot(prob.astype(BF), out, TN))
            write(first, step, 0, pair, jnp.where(lane, dq[0], dq[1]) * scale)
            grad_key, grad_value = jnp.where(lane_all, dk[0], dk[1]), jnp.where(lane_all, dv[0], dv[1])
            if total == step:
                write(0, total, 1, pair, grad_key)
                write(0, total, 2, pair, grad_value)
            else:
                acc[0] += grad_key
                acc[1] += grad_value

        if total > step:
            acc[...] = jnp.zeros(acc.shape, F32)
        for_row_blocks(total, step, block)
        if total > step:
            write(0, total, 1, pair, acc[0])
            write(0, total, 2, pair, acc[1])


def refs_by_name(names, refs):
    return SimpleNamespace(**dict(zip(names, refs, strict=True)))


def call(build, kernel, inputs, outputs, scratch, cid, **fixed):
    def body(*refs):
        kernel(refs_by_name([*inputs, *outputs, *scratch], refs), **fixed)

    results = build(
        body,
        out_shape=[jax.ShapeDtypeStruct(shape, dtype) for shape, dtype, _ in outputs.values()],
        in_specs=[spec for _, spec in inputs.values()],
        out_specs=[spec for _, _, spec in outputs.values()],
        scratch_shapes=list(scratch.values()),
        compiler_params=params(cid),
    )(*[array for array, _ in inputs.values()])
    return dict(zip(outputs, results, strict=True))


def row_blocks(cfg):
    return [slice(first, min(first + BLOCK, cfg.R)) for first in range(0, cfg.R, BLOCK)]


def normalize(x):
    center = x - jnp.mean(x, -1, keepdims=True)
    root = lax.rsqrt(jnp.mean(center * center, -1, keepdims=True) + EPS)
    return center * root, root


def norm_forward(cfg, src, gain, bias, out):
    for rows in row_blocks(cfg):
        value = (normalize(src[rows, :])[0] * gain + bias).astype(BF)
        if len(out.shape) == 2:
            out[rows, :] = value
        else:
            chunks = slice(rows.start // SLOT, rows.stop // SLOT)
            out[chunks] = value.reshape(chunks.stop - chunks.start, SLOT, cfg.D)


def norm_backward(cfg, src, gain, grad_of, total, sums, layer, which):
    by_gain = by_bias = None
    for rows in row_blocks(cfg):
        normal, root = normalize(src[rows, :])
        grad = grad_of(rows)
        scaled = grad * gain
        inner = jnp.mean(scaled * normal, -1, keepdims=True)
        total[rows, :] += root * (scaled - jnp.mean(scaled, -1, keepdims=True) - normal * inner)
        eights = (grad.shape[0] // 8, 8, grad.shape[1])
        one, two = jnp.sum((grad * normal).reshape(eights), 0), jnp.sum(grad.reshape(eights), 0)
        by_gain = one if by_gain is None else by_gain + one
        by_bias = two if by_bias is None else by_bias + two
    at = layer * 6 + which
    sums[at : at + 1, :] = jnp.sum(by_gain, 0, keepdims=True)
    sums[at + 3 : at + 4, :] = jnp.sum(by_bias, 0, keepdims=True)


def space_keys(cfg):
    row = lax.broadcasted_iota(jnp.int32, (1, cfg.R), 1)
    used = (lax.rem(row, SLOT) < cfg.PER) | (row == SLOT - 1)
    return jnp.zeros((cfg.R, 1), F32), jnp.where(used, 0.0, 1.0)


def patch_rows(cfg, rows):
    row = lax.broadcasted_iota(jnp.int32, (rows.stop - rows.start, 1), 0) + rows.start
    return lax.rem(row, SLOT) < cfg.PER


def to_all(cfg, me, copy_to, only=None):
    def send(i, carry):
        to = me ^ (cfg.N - i)
        if only is None:
            copy_to(to).start()
        else:

            @pl.when(to < only)
            def _():
                copy_to(to).start()

        return carry

    lax.fori_loop(1, cfg.N, send, 0)


def send_copy(cfg, src, dst, send, recv, to):
    return pltpu.make_async_remote_copy(src, dst, send, recv, device_id=device(cfg, to), device_id_type=MESH)


def tp_copy(src, dst, send, recv, rank):
    return pltpu.make_async_remote_copy(src, dst, send, recv, device_id={"tp": rank}, device_id_type=MESH)


def spread(cfg, me, src, dst, send, recv):
    to_all(cfg, me, lambda to: send_copy(cfg, src.at[to], dst.at[me], send, recv, to), cfg.ND)

    @pl.when(me < cfg.ND)
    def _():
        pltpu.make_async_copy(src.at[me], dst.at[me], recv).start()


def spread_sent(cfg, me, src, send):
    @pl.when(me < cfg.ND)
    def _():
        wait_bytes(src.at[pl.ds(0, cfg.ND - 1)], send)

    @pl.when(me >= cfg.ND)
    def _():
        wait_bytes(src, send)


def collect(cfg, me, src, dst, send, recv):
    to_all(cfg, me, lambda to: send_copy(cfg, src.at[to], dst.at[me], send, recv, to))
    pltpu.make_async_copy(src.at[me], dst.at[me], recv).start()


def collect_sent(cfg, me, src, send):
    @pl.when(me < cfg.ND)
    def _():
        wait_bytes(src.at[pl.ds(0, cfg.N - 1)], send)


def left_rows(cfg):
    return cfg.N * SLOT if cfg.HS == 1 else cfg.R


def head_columns(cfg, split, group):
    return (split * cfg.HG + group) * cfg.C


def swap_tp(x, out, sems):
    rank = lax.axis_index("tp")
    ranks = x.shape[0]
    local = pltpu.make_async_copy(x.at[rank], out.at[rank], sems.at[0])
    copies = [
        tp_copy(x.at[rank ^ i], out.at[rank], sems.at[i], sems.at[ranks + i], rank ^ i) for i in range(1, ranks)
    ]
    local.start()
    for copy in copies:
        copy.start()
    return [local, *copies]


def gelu(value):
    return 0.5 * value * (1.0 + lax.erf(value * 0.7071067811865476))


def gelu_slope(value):
    return 0.5 * (1.0 + lax.erf(value * 0.7071067811865476)) + value * jnp.exp(-0.5 * value * value) * 0.3989422804014327


def exchange_tp(cfg, own, full, part, from_mate, from_across, sems, work, beside, last, write):
    rank = lax.axis_index("tp")
    mate, across, far = rank ^ 1, rank ^ 2, rank ^ 3
    size = cfg.R // 2
    halves = [slice(0, size), slice(size, cfg.R)]

    def copies(h, rows):
        at = sems.at[h]
        return SimpleNamespace(
            across=tp_copy(own.at[rows], full.at[rank, rows], at.at[0], at.at[1], across),
            mate=tp_copy(own.at[rows], full.at[rank, rows], at.at[2], at.at[3], mate),
            forward=tp_copy(full.at[across, rows], full.at[across, rows], at.at[4], at.at[5], mate),
            first=tp_copy(part.at[far, rows], from_mate.at[0, rows], at.at[6], at.at[7], mate),
            second=tp_copy(part.at[mate, rows], from_mate.at[1, rows], at.at[8], at.at[9], mate),
            third=tp_copy(part.at[across, rows], from_across.at[rows], at.at[10], at.at[11], across),
        )

    both = [copies(h, rows) for h, rows in enumerate(halves)]
    for half in both:
        half.across.start()
        half.mate.start()
    full[rank] = own[...]
    for half, rows in zip(both, halves, strict=True):
        work(rank, rows)
        half.mate.wait_recv()
        work(mate, rows)
        beside()
    for half, rows in zip(both, halves, strict=True):
        half.across.wait_recv()
        half.forward.start()
        work(across, rows)
        half.forward.wait_recv()
        work(far, rows)
        half.first.start()
        half.second.start()
        beside()
        half.first.wait_recv()
        part[across, rows, :] = (part[across, rows, :].astype(F32) + from_mate[0, rows, :].astype(F32)).astype(BF)
        half.third.start()
    last()
    for half, rows in zip(both, halves, strict=True):
        half.second.wait_recv()
        half.third.wait_recv()
        near = part[rank, rows, :].astype(F32) + from_mate[1, rows, :].astype(F32)
        write(rows, near + from_across[rows, :].astype(F32))
    return [copy.wait_send for half in both for copy in vars(half).values()]


WEIGHTS = ["tqkv", "tproj", "tfc", "sqkv", "sproj", "up", "down"]


def weight_scratch(cfg):
    D, FW = cfg.D, cfg.FW
    shapes = [(D, 3 * D), (D, D), (D, D), (D, 3 * D), (D, D), (D, FW), (FW, D)]
    return {name: pltpu.VMEM(shape, BF) for name, shape in zip(WEIGHTS, shapes, strict=True)}


class Weights:
    def __init__(self, r):
        self.r, self.open = r, {}

    def load(self, layer, *names):
        for name in names:
            at = WEIGHTS.index(name)
            copy = pltpu.make_async_copy(getattr(self.r, "w_" + name).at[layer], getattr(self.r, name), self.r.w_sems.at[at])
            copy.start()
            self.open[name] = copy

    def get(self, name):
        if name in self.open:
            self.open.pop(name).wait()
        return getattr(self.r, name)


def forward_kernel(r, cfg):
    me = my_index(cfg)
    rank = lax.axis_index("tp")
    rows_t = cfg.N * SLOT
    C3 = 3 * cfg.C
    blocks = row_blocks(cfg)
    weights = Weights(r)
    weights.load(0, *WEIGHTS)
    greet_all(cfg, me)
    slot = lax.broadcasted_iota(jnp.int32, r.key.shape, 0)
    r.key[...] = (r.clip[rank] * SLOT + slot).astype(F32)
    r.space_col[...], r.space_row[...] = space_keys(cfg)
    swaps = swap_tp(r.patches, r.patch_in, r.swap_sems.at[0])
    swaps_cot = swap_tp(r.cots, r.cot_in, r.swap_sems.at[1])
    to_all(cfg, me, lambda to: send_copy(cfg, r.key, r.keys.at[me], r.key_sems.at[0], r.key_sems.at[1], to))
    pltpu.make_async_copy(r.key, r.keys.at[me], r.key_sems.at[1]).start()
    ends = []
    saves = []

    def save(src, dst):
        copy = pltpu.make_async_copy(src, dst, r.save_sems.at[len(saves)])
        copy.start()
        saves.append(copy)

    for copy in swaps:
        copy.wait()
    own_rows = cfg.R // cfg.T
    for q in range(cfg.T):
        r.x[0, q * own_rows : (q + 1) * own_rows, :] = r.patch_in[q].astype(F32)
    r.x[0, SLOT - 1 : SLOT, :] = r.cls[...].astype(F32)

    for layer in range(LAYERS):
        x, mid, after = r.x.at[layer], r.mid.at[layer], r.after.at[layer]
        att, proj, n1, so = (r.lefts.at[layer, i] for i in range(4))
        left_t = r.left_t.at[layer]
        save(x, r.o_x.at[layer])
        sems = r.time_sems.at[layer]
        gain0, bias0 = r.norms[0, layer, 0:1, :], r.norms[1, layer, 0:1, :]
        if cfg.HS == 1:
            sent = r.sent.at[layer]
            norm_forward(cfg, x, gain0, bias0, sent)
            spread(cfg, me, sent, r.got.at[layer], sems.at[0, 0], sems.at[0, 1])
            ends.append(functools.partial(spread_sent, cfg, me, sent, sems.at[0, 0]))
        else:
            norm_forward(cfg, x, gain0, bias0, left_t)
            tqkv = weights.get("tqkv")
            sent = r.sent.at[layer]
            for split in range(cfg.HS):
                first = head_columns(cfg, split, 0)
                for part in range(3):
                    value = dot(left_t[...], tqkv[:, part * cfg.D + first : part * cfg.D + first + cfg.C]).astype(BF)
                    sent[split * cfg.G : (split + 1) * cfg.G, :, part * cfg.C : (part + 1) * cfg.C] = value.reshape(
                        cfg.G, SLOT, cfg.C
                    )
            spread(cfg, me, sent, r.got.at[layer], sems.at[0, 0], sems.at[0, 1])
            ends.append(functools.partial(spread_sent, cfg, me, sent, sems.at[0, 0]))

        if layer == 0:
            wait_bytes(r.keys, r.key_sems.at[1])
            keys = r.keys[...].reshape(rows_t, 128)
            r.kcol[...] = keys[:, 0:1]
            r.krow[...] = jnp.transpose(keys)[0:1, :]
            save(r.kcol, r.o_kcol)
            save(r.krow, r.o_krow)

        tqkv = weights.get("tqkv")

        @pl.when(me < cfg.ND)
        def _(layer=layer, sems=sems, tqkv=tqkv, left_t=left_t):
            wait_bytes(r.got.at[layer], sems.at[0, 1])
            if cfg.HS == 1:
                left_t[...] = r.got[layer].reshape(rows_t, cfg.D)
            else:
                r.flat[layer, 0] = r.got[layer].reshape(rows_t, C3)
            for group in range(cfg.HG):
                flat = r.flat.at[layer, group]
                if cfg.HS == 1:
                    for part in range(3):
                        first = part * cfg.D + group * cfg.C
                        value = dot(left_t[...], tqkv[:, first : first + cfg.C])
                        flat[:, part * cfg.C : (part + 1) * cfg.C] = value.astype(BF)
                reply = r.reply.at[layer, group]

                def write(first, rows, pair, value, reply=reply):
                    chunks, columns = pl.ds(first // SLOT, rows // SLOT), slice(pair * 128, pair * 128 + 128)
                    reply[chunks, :, columns] = value.astype(BF).reshape(rows // SLOT, SLOT, 128)

                attend(flat, r.kcol, r.krow, write)
                collect(cfg, me, reply, r.back.at[layer, group], sems.at[group, 2], sems.at[group, 3])

        if cfg.HS == 1:

            @pl.when(me >= cfg.ND)
            def _(left_t=left_t):
                left_t[...] = jnp.zeros(left_t.shape, BF)

        if layer + 1 < LAYERS:
            weights.load(layer + 1, "tqkv")
        save(left_t, r.o_left_t.at[layer])
        for group in range(cfg.HG):
            ends.append(functools.partial(collect_sent, cfg, me, r.reply.at[layer, group], sems.at[group, 2]))
            save(r.flat.at[layer, group], r.o_flat.at[layer, group])

        tproj = weights.get("tproj")
        for group in range(cfg.HG):
            wait_bytes(r.back.at[layer, group], sems.at[group, 3])
            for split in range(cfg.HS):
                first = head_columns(cfg, split, group)
                value = r.back[layer, group, split * cfg.G : (split + 1) * cfg.G]
                att[:, first : first + cfg.C] = value.reshape(cfg.R, cfg.C)
        proj[...] = dot(att[...], tproj[...]).astype(BF)
        tfc = weights.get("tfc")
        value = dot(proj[...], tfc[...])
        for rows in blocks:
            mid[rows, :] = x[rows, :] + jnp.where(patch_rows(cfg, rows), value[rows, :], 0.0)
        if layer + 1 < LAYERS:
            weights.load(layer + 1, "tproj", "tfc")
        save(mid, r.o_mid.at[layer])
        norm_forward(cfg, mid, r.norms[0, layer, 1:2, :], r.norms[1, layer, 1:2, :], n1)
        sqkv = weights.get("sqkv")
        qkv = r.qkv.at[layer]
        for first in range(0, 3 * cfg.D, cfg.D):
            qkv[:, first : first + cfg.D] = dot(n1[...], sqkv[:, first : first + cfg.D]).astype(BF)
        save(qkv, r.o_qkv.at[layer])

        def write(first, rows, pair, value, so=so):
            so[pl.ds(first, rows), pair * 128 : pair * 128 + 128] = value.astype(BF)

        attend(qkv, r.space_col, r.space_row, write)
        value = dot(so[...], weights.get("sproj")[...])
        after[...] = mid[...] + value
        if layer + 1 < LAYERS:
            weights.load(layer + 1, "sqkv", "sproj")
        save(after, r.o_after.at[layer])
        save(r.lefts.at[layer], r.o_lefts.at[layer])
        norm_forward(cfg, after, r.norms[0, layer, 2:3, :], r.norms[1, layer, 2:3, :], r.n2)
        full, part = r.full.at[layer], r.part.at[layer % 2]
        up, down = weights.get("up"), weights.get("down")

        def work(q, rows, full=full, part=part, up=up, down=down):
            for first in range(0, cfg.FW, 256):
                columns = slice(first, min(first + 256, cfg.FW))
                r.hidden[rows, columns] = gelu(dot(full[q, rows, :], up[:, columns])).astype(BF)
            part[q, rows, :] = dot(r.hidden[rows, :], down[...]).astype(BF)

        def write(rows, value, after=after, layer=layer):
            value = after[rows, :] + value
            if layer + 1 < LAYERS:
                r.x[layer + 1, rows, :] = value
            else:
                r.last[rows, :] = value.astype(BF)
                if rows.start == 0:
                    r.o_out_cls[...] = r.last[SLOT - 1 : SLOT, :]

        ends += exchange_tp(
            cfg,
            r.n2,
            full,
            part,
            r.from_mate.at[layer],
            r.from_across.at[layer],
            r.tp_sems.at[layer],
            work,
            lambda: None,
            lambda full=full, layer=layer: save(full, r.o_full.at[layer]),
            write,
        )
        if layer + 1 < LAYERS:
            weights.load(layer + 1, "up", "down")
            for wait in ends:
                wait()
            ends.clear()

    for copy in swaps_cot:
        copy.wait()
    for q in range(cfg.T):
        r.grad[q * own_rows : (q + 1) * own_rows, :] = r.cot_in[q].astype(F32)
    r.grad[SLOT - 1 : SLOT, :] = r.cot_cls[...].astype(F32)
    save(r.grad, r.o_grad)
    save(r.last, r.o_last)
    for wait in ends:
        wait()
    wait_bytes(r.keys.at[pl.ds(0, cfg.N - 1)], r.key_sems.at[0])
    for copy in saves:
        copy.wait()


def forward(cfg, arrays, cid):
    D, R, L = cfg.D, cfg.R, LAYERS
    rows_t, C3 = cfg.N * SLOT, 3 * cfg.C
    wide = D if cfg.HS == 1 else C3
    own_rows = R // cfg.T
    names = ["patches", "cots", "cls", "cot_cls", "norms"]
    inputs = {name: (arrays[name], VM) for name in names}
    inputs["clip"] = (arrays["clip"], pl.BlockSpec(memory_space=pltpu.SMEM))
    inputs |= {"w_" + name: (arrays["w_" + name], ANY) for name in WEIGHTS}
    outputs = dict(
        o_x=((L, R, D), F32, ANY),
        o_mid=((L, R, D), F32, ANY),
        o_after=((L, R, D), F32, ANY),
        o_lefts=((L, 4, R, D), BF, ANY),
        o_left_t=((L, left_rows(cfg), D), BF, ANY),
        o_flat=((L, cfg.HG, rows_t, C3), BF, ANY),
        o_qkv=((L, R, 3 * D), BF, ANY),
        o_full=((L, cfg.T, R, D), BF, ANY),
        o_kcol=((rows_t, 1), F32, ANY),
        o_krow=((1, rows_t), F32, ANY),
        o_grad=((R, D), F32, ANY),
        o_last=((R, D), BF, ANY),
        o_out_cls=((1, D), BF, VM),
    )
    scratch = weight_scratch(cfg) | dict(
        patch_in=pltpu.VMEM((cfg.T, own_rows, D), BF),
        cot_in=pltpu.VMEM((cfg.T, own_rows, D), BF),
        key=pltpu.VMEM((SLOT, 128), F32),
        space_col=pltpu.VMEM((R, 1), F32),
        space_row=pltpu.VMEM((1, R), F32),
        keys=pltpu.VMEM((cfg.N, SLOT, 128), F32),
        kcol=pltpu.VMEM((rows_t, 1), F32),
        krow=pltpu.VMEM((1, rows_t), F32),
        x=pltpu.VMEM((L, R, D), F32),
        mid=pltpu.VMEM((L, R, D), F32),
        after=pltpu.VMEM((L, R, D), F32),
        last=pltpu.VMEM((R, D), BF),
        grad=pltpu.VMEM((R, D), F32),
        lefts=pltpu.VMEM((L, 4, R, D), BF),
        left_t=pltpu.VMEM((L, left_rows(cfg), D), BF),
        sent=pltpu.VMEM((L, cfg.ND, SLOT, wide), BF),
        got=pltpu.VMEM((L, cfg.N, SLOT, wide), BF),
        flat=pltpu.VMEM((L, cfg.HG, rows_t, C3), BF),
        reply=pltpu.VMEM((L, cfg.HG, cfg.N, SLOT, cfg.C), BF),
        back=pltpu.VMEM((L, cfg.HG, cfg.ND, SLOT, cfg.C), BF),
        qkv=pltpu.VMEM((L, R, 3 * D), BF),
        n2=pltpu.VMEM((R, D), BF),
        hidden=pltpu.VMEM((R, cfg.FW), BF),
        full=pltpu.VMEM((L, cfg.T, R, D), BF),
        part=pltpu.VMEM((2, cfg.T, R, D), BF),
        from_mate=pltpu.VMEM((L, 2, R, D), BF),
        from_across=pltpu.VMEM((L, R, D), BF),
        w_sems=pltpu.SemaphoreType.DMA((len(WEIGHTS),)),
        swap_sems=pltpu.SemaphoreType.DMA((2, 2 * cfg.T)),
        key_sems=pltpu.SemaphoreType.DMA((2,)),
        time_sems=pltpu.SemaphoreType.DMA((L, cfg.HG, 4)),
        tp_sems=pltpu.SemaphoreType.DMA((L, 2, 12)),
        save_sems=pltpu.SemaphoreType.DMA((4 + L * (7 + cfg.HG),)),
    )
    def build(*args, **options):
        return pl.pallas_call(*args, **options)

    return call(build, forward_kernel, inputs, outputs, scratch, cid, cfg=cfg)


def reverse(index, bits):
    return sum(((index >> bit) & 1) << (bits - 1 - bit) for bit in range(bits))


def add(a, b):
    return (a.astype(F32) + b.astype(F32)).astype(BF)


class Pipe:
    def __init__(self, stages, partners, credits, total, slots, gaps, held, every):
        self.stages, self.partners, self.credits, self.total, self.every = stages, partners, credits, total, every
        self.slots, self.gaps, self.held = slots, gaps, held
        self.jobs, self.clock = [], 0
        self.done = [[] for _ in stages]
        self.last = len(stages) - 1

    def add_jobs(self, *jobs):
        self.jobs += jobs

    def ready(self, i, k):
        if i == 0:
            if k >= len(self.jobs) or (k >= self.held and len(self.done[1]) <= k - self.held):
                return False
            if k and self.clock - self.done[0][-1] < self.every:
                return False
        elif k >= len(self.done[i - 1]) or self.clock - self.done[i - 1][k] < self.gaps[i]:
            return False
        return i == self.last or k < self.slots or len(self.done[min(i + 2, self.last)]) > k - self.slots

    def tick(self):
        self.clock += 1
        for i in reversed(range(len(self.stages))):
            k = len(self.done[i])
            if not self.ready(i, k):
                continue
            if i < self.last and k >= self.slots:
                for at, _ in self.partners(i):
                    pl.semaphore_wait(self.credits.at[at], 1)
            self.stages[i](k, self.jobs[k])
            self.done[i].append(self.clock)
            if k + self.slots < self.total:
                for sender in range(self.last):
                    if min(sender + 2, self.last) == i:
                        for at, to in self.partners(sender):
                            pl.semaphore_signal(self.credits.at[at], inc=1, device_id=to, device_id_type=MESH)

    @property
    def open(self):
        return len(self.done[-1]) < len(self.jobs)


def attn_pipe(r, cfg, total, y_first):
    S, D, T = cfg.S, cfg.D, cfg.T
    bits = S.bit_length() - 1
    rows, half = D // S, D // 2
    seq, rank = lax.axis_index("seq"), lax.axis_index("tp")
    core, chip = rank % 2, rank // 2
    held, slots = r.partial.shape[0], r.core_in.shape[0]
    seq_in = [getattr(r, f"seq_in{bit}") for bit in range(bits)]

    def remote(source, target, i, k, **to):
        return pltpu.make_async_remote_copy(
            source, target, r.sends.at[i, k % slots], r.recvs.at[i, k % slots], device_id=to, device_id_type=MESH
        )

    def part(ref, bit, mine):
        size = S >> (bit + 1)
        own = (seq >> bit) % 2
        return ref.at[pl.ds((own if mine else 1 - own) * size, size)]

    def core_copy(k):
        return remote(r.partial.at[k % held, 1 - core], r.core_in.at[k % slots], 0, k, tp=rank ^ 1)

    def x_copy(k):
        if y_first:
            return remote(r.x_in.at[k % slots, :, 1 - chip], seq_in[0].at[k % slots], 2, k, tp=rank ^ 2)
        return remote(r.core_in.at[k % slots, :, 1 - chip], r.x_in.at[k % slots], 1, k, tp=rank ^ 2)

    def bit_copy(k, bit):
        to = {"seq": seq ^ (1 << bit)}
        if bit:
            return remote(part(seq_in[bit - 1].at[k % slots], bit, False), seq_in[bit].at[k % slots], 2 + bit, k, **to)
        if y_first:
            return remote(part(r.core_in.at[k % slots], 0, False), r.x_in.at[k % slots], 1, k, **to)
        return remote(part(r.x_in.at[k % slots], 0, False), seq_in[0].at[k % slots], 2, k, **to)

    def final_copy(k, i):
        ref = r.final.at[k % slots, rank]
        return remote(ref, ref, 1 + bits + i, k, tp=rank ^ i)

    def compute(k, job):
        left, right, _, _ = job
        for side in range(2):
            value = dot(left[...], right[:, side * half : side * half + half], TN).astype(BF)
            for s in range(S):
                r.partial[k % held, side, reverse(s, bits)] = value[s * rows : (s + 1) * rows].reshape(2, rows // 2, half)
        core_copy(k).start()

    def from_core(k, job):
        core_copy(k).wait()
        r.core_in[k % slots] = add(r.core_in[k % slots], r.partial[k % held, core])
        (bit_copy(k, 0) if y_first else x_copy(k)).start()

    def from_x(k, job):
        x_copy(k).wait()
        if y_first:
            seq_in[0][k % slots] = add(seq_in[0][k % slots], r.x_in[k % slots, :, chip])
            bit_copy(k, 1).start()
        else:
            r.x_in[k % slots] = add(r.x_in[k % slots], r.core_in[k % slots, :, chip])
            bit_copy(k, 0).start()

    def from_bit(k, job, bit):
        bit_copy(k, bit).wait()
        if bit:
            target, before = seq_in[bit], seq_in[bit - 1]
        elif y_first:
            target, before = r.x_in, r.core_in
        else:
            target, before = seq_in[0], r.x_in
        value = add(target[k % slots], part(before.at[k % slots], bit, True)[...])
        if bit < bits - 1:
            target[k % slots] = value
            (x_copy(k) if bit == 0 and y_first else bit_copy(k, bit + 1)).start()
        else:
            r.final[k % slots, rank] = value[0]
            for i in range(1, T):
                final_copy(k, i).start()

    def finish(k, job):
        _, _, layer, columns = job
        for i in range(1, T):
            final_copy(k, i).wait()
        if k >= 2:
            wait_bytes(r.attn_out.at[k % 2], r.out_sems.at[k % 2])
        for q in range(T):
            at = (q // 2) * (rows // 2)
            r.attn_out[k % 2, at : at + rows // 2, (q % 2) * half : (q % 2) * half + half] = r.final[k % slots, q]
        for column, first, size in columns:
            pltpu.make_async_copy(
                r.attn_out.at[k % 2, :, pl.ds(first, size)], r.o_attn.at[layer, :, pl.ds(column, size)], r.out_sems.at[k % 2]
            ).start()

    from_bits = [functools.partial(from_bit, bit=bit) for bit in range(bits)]
    if y_first:
        stages = [compute, from_core, from_bits[0], from_x, *from_bits[1:], finish]
    else:
        stages = [compute, from_core, from_x, *from_bits, finish]

    def partners(i):
        if i == 0:
            return [(i, {"tp": rank ^ 1})]
        if i == (2 if y_first else 1):
            return [(i, {"tp": rank ^ 2})]
        if i < 2 + bits:
            return [(i, {"seq": seq ^ (1 << max(i - 2, 0))})]
        return [(1 + bits + j, {"tp": rank ^ j}) for j in range(1, T)]

    gaps = [0, 2, 8, 8 if y_first else 6] + [5] * (bits - 1) + [5]
    pipe = Pipe(stages, partners, r.credits, total, slots, gaps, held, 2)

    def flush():
        for k in range(min(2, total)):
            wait_bytes(r.attn_out.at[k], r.out_sems.at[k])

    return pipe, flush


class Pipes:
    def __init__(self, pipes, turns):
        self.pipes, self.turns = pipes, list(turns)

    def add_jobs(self, *jobs):
        for job in jobs:
            self.pipes[self.turns.pop(0)].add_jobs(job)

    def tick(self):
        for pipe in self.pipes:
            pipe.tick()

    @property
    def open(self):
        return any(pipe.open for pipe in self.pipes)


PIPE_TAGS = ["x_", "y_"]
PIPE_REFS = ["partial", "core_in", "x_in", "final", "attn_out", "sends", "recvs", "credits", "out_sems"]


def pipe_refs(r, cfg, tag):
    names = PIPE_REFS + [f"seq_in{bit}" for bit in range(cfg.S.bit_length() - 1)]
    return SimpleNamespace(o_attn=r.o_attn, **{name: getattr(r, tag + name) for name in names})


def pipe_scratch(cfg, tag, held, slots, y_first):
    S, T, D = cfg.S, cfg.T, cfg.D
    bits = S.bit_length() - 1
    rows, half = D // S, D // 2
    small = (rows // 2, half)
    types = [
        pltpu.VMEM((held, 2, S, 2) + small, BF),
        pltpu.VMEM((slots, S, 2) + small, BF),
        pltpu.VMEM((slots,) + ((S // 2, 2) if y_first else (S,)) + small, BF),
        pltpu.VMEM((slots, T) + small, BF),
        pltpu.VMEM((2, rows, D), BF),
        pltpu.SemaphoreType.DMA((1 + bits + T, slots)),
        pltpu.SemaphoreType.DMA((1 + bits + T, slots)),
        pltpu.SemaphoreType.REGULAR((1 + bits + T,)),
        pltpu.SemaphoreType.DMA((2,)),
    ]
    scratch = {tag + name: kind for name, kind in zip(PIPE_REFS, types, strict=True)}
    for bit in range(bits):
        scratch[f"{tag}seq_in{bit}"] = pltpu.VMEM((slots, S >> (bit + 1)) + small, BF)
    return scratch


def pipe_turns(cfg):
    if (cfg.D // cfg.S // 2) % 16:
        return [0] * (9 * LAYERS)
    return [0, 0, 1] * (3 * LAYERS - 1) + [0, 1, 0]


def fc_pipe(r, cfg):
    S, D, T, R = cfg.S, cfg.D, cfg.T, cfg.R
    bits = S.bit_length() - 1
    rows = D // S
    width = r.fc_part.shape[-1]
    seq = lax.axis_index("seq")
    held, slots = r.fc_part.shape[0], r.fc_in0.shape[0]
    fc_in = [getattr(r, f"fc_in{bit}") for bit in range(bits)]

    def bit_copy(k, bit):
        source = r.fc_part.at[k % held] if bit == 0 else fc_in[bit - 1].at[k % slots]
        size = S >> (bit + 1)
        other = 1 - (seq >> bit) % 2
        return pltpu.make_async_remote_copy(
            source.at[pl.ds(other * size, size)],
            fc_in[bit].at[k % slots],
            r.fc_sends.at[bit, k % slots],
            r.fc_recvs.at[bit, k % slots],
            device_id={"seq": seq ^ (1 << bit)},
            device_id_type=MESH,
        )

    def compute(k, job):
        left, right, (place, column) = job
        value = dot(left[...].reshape(T * R, D), right[:, :, column : column + width].reshape(T * R, width), TN).astype(BF)
        for s in range(S):
            r.fc_part[k % held, reverse(s, bits)] = value[s * rows : (s + 1) * rows]
        bit_copy(k, 0).start()

    def from_bit(k, job, bit):
        _, _, (place, column) = job
        bit_copy(k, bit).wait()
        size = S >> (bit + 1)
        mine = pl.ds(((seq >> bit) % 2) * size, size)
        own = r.fc_part[k % held, mine] if bit == 0 else fc_in[bit - 1][k % slots, mine]
        if bit < bits - 1:
            fc_in[bit][k % slots] = add(fc_in[bit][k % slots], own)
            bit_copy(k, bit + 1).start()
        else:
            r.o_fc[place, :, column : column + width] = own[0].astype(F32) + fc_in[bit][k % slots, 0].astype(F32)

    stages = [compute] + [functools.partial(from_bit, bit=bit) for bit in range(bits)]


    def partners(i):
        return [(i, {"seq": seq ^ (1 << i)})]

    total = 2 * LAYERS * (cfg.FW // width)
    return Pipe(stages, partners, r.fc_credits, total, slots, [0] + [7] * bits, held, 1)


STATE = ["x", "mid", "after", "flat", "qkv", "full"]


def backward_kernel(r, cfg):
    D, R, T = cfg.D, cfg.R, cfg.T
    me = my_index(cfg)
    rows_t = cfg.N * SLOT
    C, C3 = cfg.C, 3 * cfg.C
    blocks = row_blocks(cfg)
    weights = Weights(r)
    state = {}

    def load(layer, *names):
        for name in names:
            copy = pltpu.make_async_copy(getattr(r, "i_" + name).at[layer], getattr(r, name), r.state_sems.at[STATE.index(name)])
            copy.start()
            state[name] = copy

    def get(name):
        if name in state:
            state.pop(name).wait()
        return getattr(r, name)

    top = LAYERS - 1
    load_grad = pltpu.make_async_copy(r.i_grad, r.grad, r.load_sems.at[0])
    load_lefts = pltpu.make_async_copy(r.i_lefts, r.lefts, r.load_sems.at[1])
    load_grad.start()
    load(top, "full")
    weights.load(top, "up", "down")
    load(top, "after")
    weights.load(top, "sproj")
    load(top, "qkv", "mid")
    load_lefts.start()
    load_left_t = pltpu.make_async_copy(r.i_left_t, r.left_t, r.load_sems.at[2])
    load_left_t.start()
    weights.load(top, "sqkv", "tfc", "tproj", "tqkv")
    load(top, "flat", "x")
    greet_all(cfg, me)
    r.space_col[...], r.space_row[...] = space_keys(cfg)
    out_swap = swap_tp(r.i_last, r.o_out, r.swap_sems.at[0])
    turns = pipe_turns(cfg)
    made = [attn_pipe(pipe_refs(r, cfg, tag), cfg, turns.count(i), i == 1) for i, tag in enumerate(PIPE_TAGS) if i in turns]
    attn = Pipes([pipe for pipe, _ in made], turns)
    fc = fc_pipe(r, cfg)
    loaded = []

    def beside(count):
        for _ in range(count):
            fc.tick()
            attn.tick()

    load_grad.wait()
    grad = r.grad
    for layer in reversed(range(LAYERS)):
        att, proj, n1, so = (r.lefts.at[layer, i] for i in range(4))
        dqkv_t, dqkv_s = r.dqkv_t.at[layer], r.dqkv_s.at[layer]
        gt1, gt2, gu = (r.rights.at[layer, i] for i in range(3))

        r.gm[...] = grad[...].astype(BF)
        full, up, down = get("full"), weights.get("up"), weights.get("down")

        def work(q, rows, full=full, up=up, down=down):
            for first in range(0, cfg.FW, 256):
                columns = slice(first, min(first + 256, cfg.FW))
                value = dot(full[q, rows, :], up[:, columns])
                cdf = 0.5 * (1.0 + lax.erf(value * 0.7071067811865476))
                slope = cdf + value * jnp.exp(-0.5 * value * value) * 0.3989422804014327
                back = dot(r.full_grad[q, rows, :], down[columns, :], NT)
                r.hidden[q, rows, columns] = (value * cdf).astype(BF)
                r.grad_pre[q, rows, columns] = (slope * back).astype(BF)
            r.part[q, rows, :] = dot(r.grad_pre[q, rows, :], up[...], NT).astype(BF)

        def last(layer=layer):
            width = r.fc_part.shape[-1]
            for column in range(0, cfg.FW, width):
                fc.add_jobs((r.full, r.grad_pre, (layer, column)), (r.full_grad, r.hidden, (LAYERS + layer, column)))
            beside(4)

        def write(rows, value):
            r.delta[rows, :] = value

        ends = exchange_tp(
            cfg,
            r.gm,
            r.full_grad,
            r.part,
            r.from_mate,
            r.from_across,
            r.tp_sems.at[layer],
            work,
            lambda: beside(1),
            last,
            write,
        )
        for wait in ends:
            wait()
        ends.clear()
        after = get("after")
        norm_backward(cfg, after, r.norms[0, layer, 2:3, :], lambda rows: r.delta[rows, :], grad, r.sums, layer, 2)
        gu[...] = grad[...].astype(BF)
        if not loaded:
            load_lefts.wait()
            load_left_t.wait()
            loaded.append(1)
        attn.add_jobs((so, gu, layer, [(8 * D, 0, D)]))
        beside(1)

        r.gso[...] = dot(gu[...], weights.get("sproj")[...], NT).astype(BF)
        beside(1)

        def write(first, rows, part, pair, value, dqkv_s=dqkv_s):
            start = part * D + pair * 128
            dqkv_s[pl.ds(first, rows), start : start + 128] = value.astype(BF)

        for pair in range(D // 128):
            attend_back(get("qkv"), r.gso, r.space_col, r.space_row, write, r.acc, [pair])
            beside(1)
        attn.add_jobs(*[(n1, dqkv_s.at[:, pl.ds(i * D, D)], layer, [((5 + i) * D, 0, D)]) for i in range(3)])
        sqkv = weights.get("sqkv")
        r.delta[...] = sum(dot(dqkv_s[:, i * D : i * D + D], sqkv[:, i * D : i * D + D], NT) for i in range(3))
        beside(1)
        norm_backward(cfg, get("mid"), r.norms[0, layer, 1:2, :], lambda rows: r.delta[rows, :], grad, r.sums, layer, 1)
        beside(1)

        for rows in blocks:
            gt2[rows, :] = jnp.where(patch_rows(cfg, rows), grad[rows, :], 0.0).astype(BF)
        gt1[...] = dot(gt2[...], weights.get("tfc")[...], NT).astype(BF)
        attn.add_jobs((proj, gt2, layer, [(4 * D, 0, D)]), (att, gt1, layer, [(3 * D, 0, D)]))
        beside(1)
        tproj = weights.get("tproj")
        sems = r.time_sems.at[layer]
        for group in range(cfg.HG):
            for split in range(cfg.HS):
                first = head_columns(cfg, split, group)
                value = dot(gt1[...], tproj[first : first + C, :], NT).astype(BF)
                r.sent[group, split * cfg.G : (split + 1) * cfg.G] = value.reshape(cfg.G, SLOT, C)
            spread(cfg, me, r.sent.at[group], r.got.at[group], sems.at[group, 0], sems.at[group, 1])
            ends.append(functools.partial(spread_sent, cfg, me, r.sent.at[group], sems.at[group, 0]))
            beside(1)
        flat, tqkv = get("flat"), weights.get("tqkv")
        for group in range(cfg.HG):

            def write(first, rows, part, pair, value, group=group, dqkv_t=dqkv_t):
                start = part * C + pair * 128
                if cfg.HS == 1:
                    start += group * C3
                    dqkv_t[pl.ds(first, rows), start : start + 128] = value.astype(BF)
                else:
                    chunks = pl.ds(first // SLOT, rows // SLOT)
                    r.reply[0, chunks, :, start : start + 128] = value.astype(BF).reshape(rows // SLOT, SLOT, 128)

            for pair in range(C // 128):

                @pl.when(me < cfg.ND)
                def _(group=group, sems=sems, pair=pair, write=write):
                    if pair == 0:
                        wait_bytes(r.got.at[group], sems.at[group, 1])
                        r.flat_grad[...] = r.got[group].reshape(rows_t, C)
                    attend_back(flat.at[group], r.flat_grad, r.kcol, r.krow, write, r.acc, [pair])

                beside(1)
            if cfg.HS == 1:

                @pl.when(me >= cfg.ND)
                def _(group=group, dqkv_t=dqkv_t):
                    dqkv_t[:, group * C3 : (group + 1) * C3] = jnp.zeros((rows_t, C3), BF)

                columns = [(part * D + group * C, part * C, C) for part in range(3)]
                attn.add_jobs((r.left_t.at[layer], dqkv_t.at[:, pl.ds(group * C3, C3)], layer, columns))

        for group in range(cfg.HG):

            @pl.when(me < cfg.ND)
            def _(group=group, sems=sems, dqkv_t=dqkv_t, tqkv=tqkv):
                if cfg.HS == 1:
                    rows = slice(group * C, (group + 1) * C)
                    value = sum(
                        dot(dqkv_t[:, g * C3 + i * C : g * C3 + (i + 1) * C], tqkv[rows, i * D + g * C : i * D + (g + 1) * C], NT)
                        for g in range(cfg.HG)
                        for i in range(3)
                    )
                    r.reply[group] = value.astype(BF).reshape(cfg.N, SLOT, C)
                collect(cfg, me, r.reply.at[group], r.back.at[group], sems.at[group, 2], sems.at[group, 3])

            ends.append(functools.partial(collect_sent, cfg, me, r.reply.at[group], sems.at[group, 2]))
            beside(1)
        if cfg.HS == 1:
            for group in range(cfg.HG):
                beside(1)
                wait_bytes(r.back.at[group], sems.at[group, 3])
                r.delta[:, group * C : (group + 1) * C] = r.back[group].reshape(R, C).astype(F32)
        else:
            wait_bytes(r.back.at[0], sems.at[0, 3])
            for split in range(cfg.HS):
                first = head_columns(cfg, split, 0)
                for part in range(3):
                    value = r.back[0, split * cfg.G : (split + 1) * cfg.G, :, part * C : (part + 1) * C]
                    dqkv_t[:, part * D + first : part * D + first + C] = value.reshape(R, C)
            attn.add_jobs(
                *[(r.left_t.at[layer], dqkv_t.at[:, pl.ds(i * D, D)], layer, [(i * D, 0, D)]) for i in range(3)]
            )
            r.delta[...] = sum(dot(dqkv_t[:, i * D : i * D + D], tqkv[:, i * D : i * D + D], NT) for i in range(3))
        beside(1)
        norm_backward(cfg, get("x"), r.norms[0, layer, 0:1, :], lambda rows: r.delta[rows, :], grad, r.sums, layer, 0)
        while len(fc.done[0]) < len(fc.jobs):
            beside(1)
        for wait in ends:
            wait()
        if layer:
            load(layer - 1, *STATE)
            weights.load(layer - 1, *WEIGHTS)

    rest = r.sums.shape[0] - 6 * LAYERS
    if rest:
        r.sums[6 * LAYERS :, :] = jnp.zeros((rest, D), F32)

    def window(seq):
        return pl.ds(pl.multiple_of(norm_window(cfg, seq), 128), r.norm_in.shape[2])

    def norm_copy(to):
        return send_copy(
            cfg, r.sums.at[:, window(to // T)], r.norm_in.at[me], r.norm_sems.at[0], r.norm_sems.at[1], to
        )

    to_all(cfg, me, norm_copy)
    pltpu.make_async_copy(r.sums.at[:, window(lax.axis_index("seq"))], r.norm_in.at[me], r.norm_sems.at[1]).start()
    own_rows = R // T
    for q in range(T):
        r.grad_out[q] = grad[q * own_rows : (q + 1) * own_rows, :].astype(BF)
    r.o_cls[...] = grad[SLOT - 1 : SLOT, :]
    grad_swap = swap_tp(r.grad_out, r.o_grad, r.swap_sems.at[1])
    while attn.open or fc.open:
        beside(1)
    for _, flush in made:
        flush()
    wait_bytes(r.norm_in, r.norm_sems.at[1])
    r.o_norm[...] = jnp.sum(r.norm_in[...], 0)
    wait_bytes(r.norm_in.at[pl.ds(0, cfg.N - 1)], r.norm_sems.at[0])
    for copy in out_swap + grad_swap:
        copy.wait()


def norm_window(cfg, seq):
    return jnp.minimum((seq * (cfg.D // cfg.S)) // 128 * 128, cfg.D - 256)


def backward(cfg, arrays, kept, cid):
    D, R, T, L, S, FW = cfg.D, cfg.R, cfg.T, LAYERS, cfg.S, cfg.FW
    rows_t, C, C3 = cfg.N * SLOT, cfg.C, 3 * cfg.C
    own_rows = R // T
    bits = S.bit_length() - 1
    rows = D // S
    width = FW // 2
    turns = pipe_turns(cfg)
    sizes, fc_held, fc_slots = ([(2, 5), (2, 4)], 2, 4) if 1 in turns else ([(1, 2)], 1, 2)
    inputs = dict(
        norms=(arrays["norms"], VM),
        kcol=(kept["o_kcol"], VM),
        krow=(kept["o_krow"], VM),
        i_last=(kept["last"], ANY),
        i_grad=(kept["o_grad"], ANY),
        i_lefts=(kept["o_lefts"], ANY),
        i_left_t=(kept["o_left_t"], ANY),
    )
    inputs |= {"i_" + name: (kept["o_" + name], ANY) for name in STATE}
    inputs |= {"w_" + name: (arrays["w_" + name], ANY) for name in WEIGHTS}
    outputs = dict(
        o_out=((T, own_rows, D), BF, ANY),
        o_grad=((T, own_rows, D), BF, ANY),
        o_cls=((1, D), F32, VM),
        o_attn=((L, rows, 9 * D), BF, ANY),
        o_fc=((2 * L, rows, FW), F32, VM),
        o_norm=((6 * L + -6 * L % 8, 256), F32, VM),
    )
    scratch = weight_scratch(cfg) | dict(
        space_col=pltpu.VMEM((R, 1), F32),
        space_row=pltpu.VMEM((1, R), F32),
        x=pltpu.VMEM((R, D), F32),
        mid=pltpu.VMEM((R, D), F32),
        after=pltpu.VMEM((R, D), F32),
        flat=pltpu.VMEM((cfg.HG, rows_t, C3), BF),
        qkv=pltpu.VMEM((R, 3 * D), BF),
        full=pltpu.VMEM((T, R, D), BF),
        grad=pltpu.VMEM((R, D), F32),
        delta=pltpu.VMEM((R, D), F32),
        lefts=pltpu.VMEM((L, 4, R, D), BF),
        left_t=pltpu.VMEM((L, left_rows(cfg), D), BF),
        rights=pltpu.VMEM((L, 3, R, D), BF),
        dqkv_t=pltpu.VMEM((L, left_rows(cfg), 3 * D), BF),
        dqkv_s=pltpu.VMEM((L, R, 3 * D), BF),
        gm=pltpu.VMEM((R, D), BF),
        gso=pltpu.VMEM((R, D), BF),
        full_grad=pltpu.VMEM((T, R, D), BF),
        hidden=pltpu.VMEM((T, R, FW), BF),
        grad_pre=pltpu.VMEM((T, R, FW), BF),
        part=pltpu.VMEM((T, R, D), BF),
        from_mate=pltpu.VMEM((2, R, D), BF),
        from_across=pltpu.VMEM((R, D), BF),
        sent=pltpu.VMEM((cfg.HG, cfg.ND, SLOT, C), BF),
        got=pltpu.VMEM((cfg.HG, cfg.N, SLOT, C), BF),
        flat_grad=pltpu.VMEM((rows_t, C), BF),
        reply=pltpu.VMEM((cfg.HG, cfg.N, SLOT, C if cfg.HS == 1 else C3), BF),
        back=pltpu.VMEM((cfg.HG, cfg.ND, SLOT, C if cfg.HS == 1 else C3), BF),
        acc=pltpu.VMEM((2, rows_t if rows_t > 256 else 8, 128), F32),
        sums=pltpu.VMEM((6 * L + -6 * L % 8, D), F32),
        norm_in=pltpu.VMEM((cfg.N, 6 * L + -6 * L % 8, 256), F32),
        grad_out=pltpu.VMEM((T, own_rows, D), BF),
        fc_part=pltpu.VMEM((fc_held, S, rows, width), BF),
        w_sems=pltpu.SemaphoreType.DMA((len(WEIGHTS),)),
        state_sems=pltpu.SemaphoreType.DMA((len(STATE),)),
        load_sems=pltpu.SemaphoreType.DMA((3,)),
        swap_sems=pltpu.SemaphoreType.DMA((2, 2 * T)),
        time_sems=pltpu.SemaphoreType.DMA((L, cfg.HG, 4)),
        tp_sems=pltpu.SemaphoreType.DMA((L, 2, 12)),
        fc_sends=pltpu.SemaphoreType.DMA((bits, fc_slots)),
        fc_recvs=pltpu.SemaphoreType.DMA((bits, fc_slots)),
        norm_sems=pltpu.SemaphoreType.DMA((2,)),
        fc_credits=pltpu.SemaphoreType.REGULAR((bits,)),
    )
    for bit in range(bits):
        scratch[f"fc_in{bit}"] = pltpu.VMEM((fc_slots, S >> (bit + 1), rows, width), BF)
    def build(*args, **options):
        return pl.pallas_call(*args, **options)

    for i, tag in enumerate(PIPE_TAGS):
        if i in turns:
            scratch |= pipe_scratch(cfg, tag, *sizes[i], i == 1)
    return call(build, backward_kernel, inputs, outputs, scratch, cid, cfg=cfg)


def shards(
    cfg,
    patches,
    cls_tokens,
    frame_clip,
    norm_gain,
    norm_bias,
    w_tqkv,
    w_tproj,
    w_tfc,
    w_sqkv,
    w_sproj,
    w_fc1,
    w_fc2,
    cot_patches,
    cot_cls,
):
    frames, local, D = patches.shape
    groups = local // cfg.PER
    def padded(x):
        x = x.reshape(frames, groups, cfg.PER, D)
        return jnp.pad(x, ((0, 0), (0, 0), (0, SLOT - cfg.PER), (0, 0))).reshape(frames, groups * SLOT, D)

    arrays = dict(
        patches=padded(patches),
        cots=padded(cot_patches),
        cls=cls_tokens,
        cot_cls=cot_cls,
        clip=frame_clip,
        norms=jnp.stack([norm_gain, norm_bias]),
        w_tqkv=w_tqkv,
        w_tproj=w_tproj,
        w_tfc=w_tfc,
        w_sqkv=w_sqkv,
        w_sproj=w_sproj,
        w_up=w_fc1,
        w_down=w_fc2,
    )
    kept = forward(cfg, arrays, 0)
    kept["last"] = kept["o_last"].reshape(cfg.T, -1, D)
    out = backward(cfg, arrays, kept, 1)

    def unpadded(x):
        return x.reshape(frames, groups, SLOT, D)[:, :, : cfg.PER].reshape(frames, local, D)

    rows = D // cfg.S
    seq = lax.axis_index("seq")
    norm = lax.dynamic_slice_in_dim(out["o_norm"][: 6 * LAYERS], seq * rows - norm_window(cfg, seq), rows, 1)
    fc = out["o_fc"]
    return (
        unpadded(out["o_out"]),
        kept["o_out_cls"],
        unpadded(out["o_grad"]).astype(F32),
        out["o_cls"],
        out["o_attn"].astype(F32),
        norm.reshape(LAYERS, 6, rows),
        fc[:LAYERS],
        jnp.swapaxes(fc[LAYERS:], 1, 2),
    )


def solution(mesh):
    S, T = mesh.shape["seq"], mesh.shape["tp"]

    def run(*args):
        local, D, FW = args[0].shape[1] // T, args[0].shape[2], args[10].shape[2] // T
        per = max(n for n in range(1, SLOT) if local % n == 0)
        groups = args[0].shape[1] // per
        pairs = D // (2 * HEAD_DIM)
        splits = max(n for n in range(1, pairs + 1) if pairs % n == 0 and (n == 1 or groups * n <= S * T))
        head_groups = 3 if splits == 1 and pairs % 3 == 0 else 1
        cfg = Cfg(
            S, T, S * T, D, groups, groups * SLOT, per, splits, groups * splits, head_groups, D // (splits * head_groups), FW
        )
        return jax.shard_map(
            functools.partial(shards, cfg),
            mesh=mesh,
            in_specs=(
                P("seq", "tp", None),
                P(("seq", "tp"), None),
                P("seq"),
                P(),
                P(),
                P(),
                P(),
                P(),
                P(),
                P(),
                P(None, None, "tp"),
                P(None, "tp", None),
                P("seq", "tp", None),
                P(("seq", "tp"), None),
            ),
            out_specs=(
                P("seq", "tp", None),
                P(("seq", "tp"), None),
                P("seq", "tp", None),
                P(("seq", "tp"), None),
                P(None, "seq", None),
                P(None, None, "seq"),
                P(None, "seq", "tp"),
                P(None, "tp", "seq"),
            ),
            check_vma=False,
        )(*args)

    return run
```

profile of v0, /device:TPU:0, one launch (start us, length us, event | category | flops | bytes accessed | tf_op | source)
XLA Modules:
  0.0 349.1 jit_solution(54783150180529586)
XLA Ops:
  0.6 0.8 copy_bitcast_fusion
  1.4 0.6 pad_maximum_fusion.refs_4_.refs_0_
  2.0 1.0 copy.30
  3.0 1.0 copy.31
  4.0 1.0 pad_bitcast_fusion
  5.0 107.3 %shard_map.197 = (f32[2,224,768]{2,1,0:T(8,128)}, f32[2,224,768]{2,1,0:T(8,128)}, f32[2,224,768]{2,1,0:T(8,128)}, bf16[2,4,224,768]{3,2,1,0:T(8,128)(2,1)}, bf16...) custom-call(bf16[4,56,768]{2,1,0:T(8,128)(2,1)} %get-tuple-element.5, ...), custom_call_target="tpu_custom_call" | custom-call | tf_op jit(solution)/shard_map/pallas_call | solution.py:166
  112.3 226.9 %shard_map.198 = (bf16[4,56,768]{2,1,0:T(8,128)(2,1)}, bf16[4,56,768]{2,1,0:T(8,128)(2,1)}, f32[1,768]{1,0:T(1,128)}, bf16[2,96,6912]{2,1,0:T(8,128)(2,1)}, f32[4,96,768]{2,1,0:T(8,128)}, /*index=5*/f32[16,256]{1,0:T(8,128)}) custom-call(f32[2,2,3,768]{3,2,1,0:T(4,128)} %pad_maximum_fusion.refs_4_.refs_0_, f32[256,1]{1,0:T(8,128)} %get-tuple-element.27.refs_1_, ...), custom_call_target="tpu_custom_call" | custom-call | tf_op jit(solution)/shard_map/pallas_call | solution.py:166
  339.2 0.0 copy-start.2
  339.2 4.5 %convert_element_type.14 = f32[2,96,6912]{2,1,0:T(8,128)} convert(bf16[2,96,6912]{2,1,0:T(8,128)(2,1)} %get-tuple-element.43) | non-fusion elementwise | flops 1327104 | bytes 7962624 | tf_op jit(solution)/shard_map/convert_element_type | solution.py:1290
  343.7 0.0 copy-start
  343.7 0.0 copy-start.1
  343.7 0.0 copy-done.2
  343.8 0.0 copy-start.3
  343.8 0.0 copy-start.4
  343.8 0.0 copy-start.5
  343.8 1.1 copy.33
  344.8 0.2 copy-done
  345.0 1.1 slice_bitcast_fusion
  346.1 0.0 copy-done.1
  346.1 0.8 copy.32
  346.9 0.0 copy-done.3
  346.9 0.1 constant_dynamic-slice_fusion
  347.0 0.6 copy.34
  347.6 0.0 copy-done.4
  347.6 0.6 copy.39
  348.2 0.0 copy-done.5
  348.2 0.6 copy.40
  (2 shorter events, 0.1 us)
Async XLA Ops:
  339.2 4.5 %copy-start.2 = (bf16[4,56,768]{2,1,0:T(8,128)(2,1)S(1)}, bf16[4,56,768]{2,1,0:T(8,128)(2,1)}, u32[]{:S(2)}) copy-start(bf16[4,56,768]{2,1,0:T(8,128)(2,1)} %get-tuple-element.41) | copy-start | bytes 1032196
  343.7 1.3 copy-start
  343.7 2.4 copy-start.1
  343.8 3.2 copy-start.3
  343.8 3.9 %copy-start.4 = (bf16[1,768]{1,0:T(2,128)(2,1)S(1)}, bf16[1,768]{1,0:T(2,128)(2,1)}, u32[]{:S(2)}) copy-start(bf16[1,768]{1,0:T(2,128)(2,1)} %get-tuple-element.69) | copy-start | bytes 4612
  343.8 4.4 %copy-start.5 = (f32[1,768]{1,0:T(1,128)S(1)}, f32[1,768]{1,0:T(1,128)}, u32[]{:S(2)}) copy-start(f32[1,768]{1,0:T(1,128)} %get-tuple-element.71) | copy-start | bytes 9220
where the time goes:
time: 353 us; the launch traced here: 349 us
  Pallas kernels  334 us (95%)
  local copies, waits for them, and re-layouts  8.73 us (2%)
  other arithmetic  5.2 us (1%)
    pallas_call x2, Pallas kernels, call(): build(body, out_shape=[jax.ShapeDtypeStruct(shape, dtype) for shape, dtyp...  334 us

commit v1 on v0

--- a/solution.py
+++ b/solution.py
@@ -70,11 +70,11 @@
     return ref[rows, start : start + 128]
 
 
-def softmax_rows(query, key, mask):
+def weights_of(query, key, mask):
     scores = jnp.where(mask, dot(query, key, NT), NEG_FILL)
     top = jnp.max(scores, -1, keepdims=True)
     weight = jnp.exp(scores - top)
-    return weight * (1.0 / jnp.sum(weight, -1, keepdims=True))
+    return weight, jnp.sum(weight, -1, keepdims=True), top
 
 
 def for_row_blocks(total, step, block):
@@ -89,7 +89,7 @@
         lax.fori_loop(0, total // step, body, 0)
 
 
-def attend(qkv, kcol, krow, write):
+def attend(qkv, kcol, krow, write, lse, heads):
     total, width = qkv.shape[0], qkv.shape[1] // 3
     step = total if total <= 256 else 64
     every = slice(0, total)
@@ -103,14 +103,18 @@
             query = head_pair(qkv, rows, width, 0, pair) * jnp.asarray(HEAD_DIM**-0.5, BF)
             key = head_pair(qkv, every, width, 1, pair)
             value = head_pair(qkv, every, width, 2, pair)
-            prob0 = softmax_rows(jnp.where(lane, query, zero), key, mask).astype(BF)
-            prob1 = softmax_rows(jnp.where(lane, zero, query), key, mask).astype(BF)
-            write(first, step, pair, jnp.where(lane, dot(prob0, value), dot(prob1, value)))
+            outs = []
+            for half, own in enumerate((jnp.where(lane, query, zero), jnp.where(lane, zero, query))):
+                weight, total_weight, top = weights_of(own, key, mask)
+                outs.append(dot((weight * (1.0 / total_weight)).astype(BF), value))
+                at = heads + 2 * pair + half
+                lse[rows, at : at + 1] = top + jnp.log(total_weight)
+            write(first, step, pair, jnp.where(lane, outs[0], outs[1]))
 
     for_row_blocks(total, step, block)
 
 
-def attend_back(qkv, grad, kcol, krow, write, acc, pairs):
+def attend_back(qkv, grad, kcol, krow, write, acc, pairs, lse, heads):
     total, width = qkv.shape[0], qkv.shape[1] // 3
     step = total if total <= 256 else 64
     every = slice(0, total)
@@ -129,9 +133,10 @@
             query = head_pair(qkv, rows, width, 0, pair) * jnp.asarray(scale, BF)
             out = grad[rows, pair * 128 : pair * 128 + 128]
             dq, dk, dv = [], [], []
-            for lower in (True, False):
-                own = (lambda v: jnp.where(lane, v, zero)) if lower else (lambda v: jnp.where(lane, zero, v))
-                prob = softmax_rows(own(query), key, mask)
+            for half in range(2):
+                own = (lambda v: jnp.where(lane, zero, v)) if half else (lambda v: jnp.where(lane, v, zero))
+                at = heads + 2 * pair + half
+                prob = jnp.exp(jnp.where(mask, dot(own(query), key, NT), NEG_FILL) - lse[rows, at : at + 1])
                 back = dot(own(out), value, NT)
                 delta = jnp.sum(prob * back, -1, keepdims=True)
                 score = (prob * (back - delta)).astype(BF)
@@ -465,7 +470,7 @@
                     chunks, columns = pl.ds(first // SLOT, rows // SLOT), slice(pair * 128, pair * 128 + 128)
                     reply[chunks, :, columns] = value.astype(BF).reshape(rows // SLOT, SLOT, 128)
 
-                attend(flat, r.kcol, r.krow, write)
+                attend(flat, r.kcol, r.krow, write, r.lse_t.at[layer], group * (cfg.C // HEAD_DIM))
                 collect(cfg, me, reply, r.back.at[layer, group], sems.at[group, 2], sems.at[group, 3])
 
         if cfg.HS == 1:
@@ -477,6 +482,7 @@
         if layer + 1 < LAYERS:
             weights.load(layer + 1, "tqkv")
         save(left_t, r.o_left_t.at[layer])
+        save(r.lse_t.at[layer], r.o_lse_t.at[layer])
         for group in range(cfg.HG):
             ends.append(functools.partial(collect_sent, cfg, me, r.reply.at[layer, group], sems.at[group, 2]))
             save(r.flat.at[layer, group], r.o_flat.at[layer, group])
@@ -506,7 +512,8 @@
         def write(first, rows, pair, value, so=so):
             so[pl.ds(first, rows), pair * 128 : pair * 128 + 128] = value.astype(BF)
 
-        attend(qkv, r.space_col, r.space_row, write)
+        attend(qkv, r.space_col, r.space_row, write, r.lse_s.at[layer], 0)
+        save(r.lse_s.at[layer], r.o_lse_s.at[layer])
         value = dot(so[...], weights.get("sproj")[...])
         after[...] = mid[...] + value
         if layer + 1 < LAYERS:
@@ -580,6 +587,8 @@
         o_after=((L, R, D), F32, ANY),
         o_lefts=((L, 4, R, D), BF, ANY),
         o_left_t=((L, left_rows(cfg), D), BF, ANY),
+        o_lse_t=((L, rows_t, 128), F32, ANY),
+        o_lse_s=((L, R, 128), F32, ANY),
         o_flat=((L, cfg.HG, rows_t, C3), BF, ANY),
         o_qkv=((L, R, 3 * D), BF, ANY),
         o_full=((L, cfg.T, R, D), BF, ANY),
@@ -605,6 +614,8 @@
         grad=pltpu.VMEM((R, D), F32),
         lefts=pltpu.VMEM((L, 4, R, D), BF),
         left_t=pltpu.VMEM((L, left_rows(cfg), D), BF),
+        lse_t=pltpu.VMEM((L, rows_t, 128), F32),
+        lse_s=pltpu.VMEM((L, R, 128), F32),
         sent=pltpu.VMEM((L, cfg.ND, SLOT, wide), BF),
         got=pltpu.VMEM((L, cfg.N, SLOT, wide), BF),
         flat=pltpu.VMEM((L, cfg.HG, rows_t, C3), BF),
@@ -622,7 +633,7 @@
         key_sems=pltpu.SemaphoreType.DMA((2,)),
         time_sems=pltpu.SemaphoreType.DMA((L, cfg.HG, 4)),
         tp_sems=pltpu.SemaphoreType.DMA((L, 2, 12)),
-        save_sems=pltpu.SemaphoreType.DMA((4 + L * (7 + cfg.HG),)),
+        save_sems=pltpu.SemaphoreType.DMA((4 + L * (9 + cfg.HG),)),
     )
     def build(*args, **options):
         return pl.pallas_call(*args, **options)
@@ -903,7 +914,7 @@
     return Pipe(stages, partners, r.fc_credits, total, slots, [0] + [7] * bits, held, 1)
 
 
-STATE = ["x", "mid", "after", "flat", "qkv", "full"]
+STATE = ["x", "mid", "after", "flat", "qkv", "full", "lse_t", "lse_s"]
 
 
 def backward_kernel(r, cfg):
@@ -934,12 +945,12 @@
     weights.load(top, "up", "down")
     load(top, "after")
     weights.load(top, "sproj")
-    load(top, "qkv", "mid")
+    load(top, "qkv", "lse_s", "mid")
     load_lefts.start()
     load_left_t = pltpu.make_async_copy(r.i_left_t, r.left_t, r.load_sems.at[2])
     load_left_t.start()
     weights.load(top, "sqkv", "tfc", "tproj", "tqkv")
-    load(top, "flat", "x")
+    load(top, "flat", "lse_t", "x")
     greet_all(cfg, me)
     r.space_col[...], r.space_row[...] = space_keys(cfg)
     out_swap = swap_tp(r.i_last, r.o_out, r.swap_sems.at[0])
@@ -1017,8 +1028,9 @@
             start = part * D + pair * 128
             dqkv_s[pl.ds(first, rows), start : start + 128] = value.astype(BF)
 
+        lse_s = get("lse_s")
         for pair in range(D // 128):
-            attend_back(get("qkv"), r.gso, r.space_col, r.space_row, write, r.acc, [pair])
+            attend_back(get("qkv"), r.gso, r.space_col, r.space_row, write, r.acc, [pair], lse_s, 0)
             beside(1)
         attn.add_jobs(*[(n1, dqkv_s.at[:, pl.ds(i * D, D)], layer, [((5 + i) * D, 0, D)]) for i in range(3)])
         sqkv = weights.get("sqkv")
@@ -1042,7 +1054,7 @@
             spread(cfg, me, r.sent.at[group], r.got.at[group], sems.at[group, 0], sems.at[group, 1])
             ends.append(functools.partial(spread_sent, cfg, me, r.sent.at[group], sems.at[group, 0]))
             beside(1)
-        flat, tqkv = get("flat"), weights.get("tqkv")
+        flat, lse_t, tqkv = get("flat"), get("lse_t"), weights.get("tqkv")
         for group in range(cfg.HG):
 
             def write(first, rows, part, pair, value, group=group, dqkv_t=dqkv_t):
@@ -1061,7 +1073,8 @@
                     if pair == 0:
                         wait_bytes(r.got.at[group], sems.at[group, 1])
                         r.flat_grad[...] = r.got[group].reshape(rows_t, C)
-                    attend_back(flat.at[group], r.flat_grad, r.kcol, r.krow, write, r.acc, [pair])
+                    heads = group * (C // HEAD_DIM)
+                    attend_back(flat.at[group], r.flat_grad, r.kcol, r.krow, write, r.acc, [pair], lse_t, heads)
 
                 beside(1)
             if cfg.HS == 1:
@@ -1184,6 +1197,8 @@
         mid=pltpu.VMEM((R, D), F32),
         after=pltpu.VMEM((R, D), F32),
         flat=pltpu.VMEM((cfg.HG, rows_t, C3), BF),
+        lse_t=pltpu.VMEM((rows_t, 128), F32),
+        lse_s=pltpu.VMEM((R, 128), F32),
         qkv=pltpu.VMEM((R, 3 * D), BF),
         full=pltpu.VMEM((T, R, D), BF),
         grad=pltpu.VMEM((R, D), F32),

time: 353 us -> 352 us (level)
  no operation moved by 1% of the time
where the time goes in v1:
time: 352 us; the launch traced here: 348 us
  Pallas kernels  333 us (95%)
  local copies, waits for them, and re-layouts  8.73 us (2%)
  other arithmetic  5.2 us (1%)
    pallas_call x2, Pallas kernels, call(): build(body, out_shape=[jax.ShapeDtypeStruct(shape, dtype) for shape, dtyp...  333 us

profile of v1, /device:TPU:0, one launch (start us, length us, event | category | flops | bytes accessed | tf_op | source)
XLA Modules:
  0.0 348.2 jit_solution(4678845137792093598)
XLA Ops:
  0.6 0.8 copy_bitcast_fusion
  1.4 0.6 pad_maximum_fusion.refs_4_.refs_0_
  2.0 1.0 copy.30
  3.0 1.0 copy.31
  4.0 1.0 pad_bitcast_fusion
  5.0 106.3 %shard_map.197 = (f32[2,224,768]{2,1,0:T(8,128)}, f32[2,224,768]{2,1,0:T(8,128)}, f32[2,224,768]{2,1,0:T(8,128)}, bf16[2,4,224,768]{3,2,1,0:T(8,128)(2,1)}, bf16...) custom-call(bf16[4,56,768]{2,1,0:T(8,128)(2,1)} %get-tuple-element.6, ...), custom_call_target="tpu_custom_call" | custom-call | tf_op jit(solution)/shard_map/pallas_call | solution.py:171
  111.3 226.8 %shard_map.198 = (bf16[4,56,768]{2,1,0:T(8,128)(2,1)}, bf16[4,56,768]{2,1,0:T(8,128)(2,1)}, f32[1,768]{1,0:T(1,128)}, bf16[2,96,6912]{2,1,0:T(8,128)(2,1)}, f32[4,96,768]{2,1,0:T(8,128)}, /*index=5*/f32[16,256]{1,0:T(8,128)}) custom-call(f32[2,2,3,768]{3,2,1,0:T(4,128)} %pad_maximum_fusion.refs_4_.refs_0_, f32[256,1]{1,0:T(8,128)} %get-tuple-element.29.refs_1_, ...), custom_call_target="tpu_custom_call" | custom-call | tf_op jit(solution)/shard_map/pallas_call | solution.py:171
  338.1 0.0 copy-start.2
  338.1 4.5 %convert_element_type.14 = f32[2,96,6912]{2,1,0:T(8,128)} convert(bf16[2,96,6912]{2,1,0:T(8,128)(2,1)} %get-tuple-element.47) | non-fusion elementwise | flops 1327104 | bytes 7962624 | tf_op jit(solution)/shard_map/convert_element_type | solution.py:1305
  342.6 0.0 copy-start
  342.6 0.0 copy-start.1
  342.6 0.0 copy-done.2
  342.7 0.0 copy-start.3
  342.7 0.0 copy-start.4
  342.7 0.0 copy-start.5
  342.7 1.1 copy.33
  343.8 0.2 copy-done
  343.9 1.1 slice_bitcast_fusion
  345.0 0.0 copy-done.1
  345.0 0.8 copy.32
  345.9 0.0 copy-done.3
  345.9 0.1 constant_dynamic-slice_fusion
  346.0 0.6 copy.34
  346.6 0.0 copy-done.4
  346.6 0.6 copy.39
  347.1 0.0 copy-done.5
  347.1 0.6 copy.40
  (2 shorter events, 0.1 us)
Async XLA Ops:
  338.1 4.5 %copy-start.2 = (bf16[4,56,768]{2,1,0:T(8,128)(2,1)S(1)}, bf16[4,56,768]{2,1,0:T(8,128)(2,1)}, u32[]{:S(2)}) copy-start(bf16[4,56,768]{2,1,0:T(8,128)(2,1)} %get-tuple-element.45) | copy-start | bytes 1032196
  342.6 1.3 copy-start
  342.6 2.4 copy-start.1
  342.7 3.2 copy-start.3
  342.7 3.9 %copy-start.4 = (bf16[1,768]{1,0:T(2,128)(2,1)S(1)}, bf16[1,768]{1,0:T(2,128)(2,1)}, u32[]{:S(2)}) copy-start(bf16[1,768]{1,0:T(2,128)(2,1)} %get-tuple-element.73) | copy-start | bytes 4612
  342.7 4.4 %copy-start.5 = (f32[1,768]{1,0:T(1,128)S(1)}, f32[1,768]{1,0:T(1,128)}, u32[]{:S(2)}) copy-start(f32[1,768]{1,0:T(1,128)} %get-tuple-element.75) | copy-start | bytes 9220
